TPU v7x, 32 devices: a whole 2x2x4 slice. The times are simulated.
32 devices in a mesh: grp: 2 (over y), gx: 4 (over z), gy: 2 (over x), gz: 2 (over core).
Axes of the slice: x: 2, y: 2, z: 4, core: 2. Of those that a mesh axis runs over, the one named last changes fastest.
Arguments:
- tokens: bfloat16 [128, 6144], P(('grp', 'gx'), ('gy', 'gz')), parts along dimension 0, may hold values from -6 to 6
- w_gate: bfloat16 [6144, 14336], P(('gy', 'gz'), 'gx'), may hold values from -0.078125 to 0.078125
- w_up: bfloat16 [6144, 14336], P(('gy', 'gz'), 'gx'), may hold values from -0.078125 to 0.078125
- w_down: bfloat16 [14336, 6144], P('gx', ('gy', 'gz')), may hold values from -0.046875 to 0.046875
- grad_out: bfloat16 [128, 6144], P(('grp', 'gx'), ('gy', 'gz')), parts along dimension 0, may hold values from -2.5 to 2.5
Outputs:
- mixed: bfloat16 [128, 6144], P(('grp', 'gx'), ('gy', 'gz')), parts along dimension 0
- grad_tokens: bfloat16 [128, 6144], P(('grp', 'gx'), ('gy', 'gz')), parts along dimension 0
- grad_gate: bfloat16 [12288, 14336], P(('grp', 'gy', 'gz'), 'gx'), parts along dimension 0
- grad_up: bfloat16 [12288, 14336], P(('grp', 'gy', 'gz'), 'gx'), parts along dimension 0
- grad_down: bfloat16 [28672, 6144], P(('grp', 'gx'), ('gy', 'gz')), parts along dimension 0
There are 2 independent parts, one for each index of `grp`. A program takes and returns all parts, laid end to end along the dimension named above; an argument that names none is the same for every part. Nothing has to cross between parts.
All inputs are finite; a program needn't handle non-finite values.
Results may differ from a plain program's by a relative error of at most 0.0051.
Values may be sent and summed in bfloat16 or wider, within the bound.
A program may use at most 192 MiB of HBM per device.

v0:
```python
import jax
import jax.numpy as jnp
from jax import lax
from jax.sharding import PartitionSpec as P


def gate_slope(gate_pre):
    sig = jax.nn.sigmoid(gate_pre)
    return sig * (1.0 + gate_pre * (1.0 - sig))


def inner_last(left, right):
    return lax.dot_general(
        left, right, (((1,), (1,)), ((), ())), preferred_element_type=jnp.float32
    )


def inner_first(left, right):
    return lax.dot_general(
        left, right, (((0,), (0,)), ((), ())), preferred_element_type=jnp.float32
    )


def local(tokens, w_gate, w_up, w_down, grad_out):
    piece = lax.all_gather(tokens, "gx", axis=0, tiled=True)
    gate_pre = jnp.dot(piece, w_gate, preferred_element_type=jnp.float32)
    up_pre = jnp.dot(piece, w_up, preferred_element_type=jnp.float32)
    gathered = piece
    gate_pre, up_pre = lax.psum((gate_pre, up_pre), ("gy", "gz"))
    act_gate = jax.nn.silu(gate_pre)
    hidden = (act_gate * up_pre).astype(jnp.bfloat16)
    rows_hidden = hidden
    mixed = lax.psum_scatter(
        jnp.dot(rows_hidden, w_down, preferred_element_type=jnp.float32),
        "gx",
        scatter_dimension=0,
        tiled=True,
    ).astype(jnp.bfloat16)
    piece = lax.all_gather(grad_out, "gx", axis=0, tiled=True)
    rows_grad = inner_last(piece, w_down)
    part_hidden = rows_grad
    rows_hidden = hidden
    part_hidden, acc_down = (part_hidden, inner_first(rows_hidden, piece))
    grad_down = acc_down.astype(jnp.bfloat16)
    grad_hidden = lax.psum(part_hidden, ("gy", "gz"))
    pre_gate = (grad_hidden * up_pre * gate_slope(gate_pre)).astype(jnp.bfloat16)
    pre_up = (grad_hidden * act_gate).astype(jnp.bfloat16)
    acc_gate = inner_first(gathered, pre_gate)
    acc_up = inner_first(gathered, pre_up)
    grad_tokens = lax.psum_scatter(
        inner_last(pre_gate, w_gate) + inner_last(pre_up, w_up),
        "gx",
        scatter_dimension=0,
        tiled=True,
    ).astype(jnp.bfloat16)
    return (
        mixed,
        grad_tokens,
        acc_gate.astype(jnp.bfloat16),
        acc_up.astype(jnp.bfloat16),
        grad_down,
    )


def solution(mesh):
    return jax.shard_map(
        local,
        mesh=mesh,
        in_specs=(
            P(("grp", "gx"), ("gy", "gz")),
            P(("gy", "gz"), "gx"),
            P(("gy", "gz"), "gx"),
            P("gx", ("gy", "gz")),
            P(("grp", "gx"), ("gy", "gz")),
        ),
        out_specs=(
            P(("grp", "gx"), ("gy", "gz")),
            P(("grp", "gx"), ("gy", "gz")),
            P(("grp", "gy", "gz"), "gx"),
            P(("grp", "gy", "gz"), "gx"),
            P(("grp", "gx"), ("gy", "gz")),
        ),
        check_vma=False,
    )
```

profile of v0, /device:TPU:0, one launch (start us, length us, event | category | flops | bytes accessed | tf_op | source)
XLA Modules:
  0.0 196.9 jit_solution(308624683116563377)
XLA Ops:
  7.2 0.0 all-reduce.3.cloned.1.call-start
  7.2 0.0 copy-start
  7.2 15.8 %all_gather.6 = bf16[64,1536]{1,0:T(8,128)(2,1)S(1)} all-gather(bf16[16,1536]{1,0:T(8,128)(2,1)} %param.5), channel_id=1, replica_groups=mesh['grp'=2,'gx'=4,'gy'=2,'gz'=2] {'gx'}, dimensions={0}, use_global_device_ids=true | all-gather | bytes 245760 | tf_op jit(solution)/shard_map/all_gather | solution.py:25
  23.0 0.0 slice-start
  23.0 0.0 slice-start.1
  23.0 7.2 %fusion.4 = f32[64,3584]{1,0:T(8,128)} fusion(bf16[64,1536]{1,0:T(8,128)(2,1)S(1)} %all_gather.6, bf16[1536,3584]{1,0:T(8,128)(2,1)} %param.7), kind=kOutput, calls=%fused_computation.12 | convolution fusion | flops 704643072 | bytes 12124160 | tf_op jit(solution)/shard_map/dot_general | solution.py:27
  30.2 0.0 copy-done
  30.2 0.0 copy-start.1
  30.2 2.9 %fusion.3 = f32[64,3584]{1,0:T(8,128)} fusion(bf16[64,1536]{1,0:T(8,128)(2,1)S(1)} %all_gather.6, bf16[1536,3584]{1,0:T(8,128)(2,1)S(1)} %copy-done), kind=kOutput, calls=%fused_computation.11 | convolution fusion | flops 704643072 | bytes 12124160 | tf_op jit(solution)/shard_map/dot_general | solution.py:26
  33.2 0.0 copy-done.1
  33.2 14.0 %all_gather.7 = bf16[64,1536]{1,0:T(8,128)(2,1)S(1)} all-gather(bf16[16,1536]{1,0:T(8,128)(2,1)S(1)} %copy-done.1), channel_id=1, replica_groups=mesh['grp'=2,'gx'=4,'gy'=2,'gz'=2] {'gx'}, dimensions={0}, use_global_device_ids=true | all-gather | bytes 245760 | tf_op jit(solution)/shard_map/all_gather | solution.py:39
  47.2 0.0 slice-done
  47.2 0.0 slice-done.1
  47.2 0.0 slice-done.2
  47.2 4.3 %fusion.6 = f32[64,3584]{1,0:T(8,128)} fusion(bf16[64,1536]{1,0:T(8,128)(2,1)S(1)} %all_gather.7, bf16[3584,1536]{1,0:T(8,128)(2,1)S(1)} %bitcast.23), kind=kOutput, calls=%fused_computation.14 | convolution fusion | flops 704643072 | bytes 12124160 | tf_op jit(solution)/shard_map/dot_general | solution.py:13
  51.6 0.0 all-reduce.3.cloned.1.call-update
  51.6 0.0 reduce-scatter.3.cloned.1.call-start
  51.7 63.5 %all-reduce.3.cloned.1.call-done = (f32[64,3584]{1,0:T(8,128)}, f32[64,3584]{1,0:T(8,128)}, f32[64,3584]{1,0:T(8,128)}) async-done(((f32[64,3584]{1,0:T(8,128)}, f32[64,3584]{1,0:T(8,128)}, f32[64,3584]{1,0:T(8,128)}), (f32[64,3584]{1,0:T(8,128)}, f32[64,3584]{1,0:T(8,128)}, f32[64,3584]{1,0:T(8,128)})) %all-reduce.3.cloned.1.call-update) | async-done | bytes 2752528 | tf_op jit(solution)/shard_map/psum | solution.py:29
  115.2 2.2 %multiply_convert_fusion = (bf16[64,3584]{1,0:T(8,128)(2,1)S(1)}, bf16[64,3584]{1,0:T(8,128)(2,1)S(1)}, bf16[64,3584]{1,0:T(8,128)(2,1)S(1)}) fusion(f32[64,3584]{1,0:T(8,128)} %get-tuple-element.12, f32[64,3584]{1,0:T(8,128)} %get-tuple-element.11, f32[64,3584]{1,0:T(8,128)} %get-tuple-element.10), kind=kLoop, calls=%fused_computation.6 | loop fusion | flops 3440640 | bytes 4128768 | tf_op jit(solution)/shard_map/convert_element_type | solution.py:47
  117.4 6.9 %fusion.5 = f32[64,1536]{1,0:T(8,128)} fusion(bf16[64,3584]{1,0:T(8,128)(2,1)S(1)} %get-tuple-element.15, bf16[3584,1536]{1,0:T(8,128)(2,1)} %param.8), kind=kOutput, calls=%fused_computation.13 | convolution fusion | flops 704643072 | bytes 11862016 | tf_op jit(solution)/shard_map/dot_general | solution.py:34
  124.3 0.0 reduce-scatter.3.cloned.1.call-update
  124.3 0.2 reduce-scatter.5.cloned.1.call-start
  124.5 7.5 %fusion.7 = f32[64,1536]{1,0:T(8,128)S(1)} fusion(bf16[64,3584]{1,0:T(8,128)(2,1)S(1)} %get-tuple-element.14, bf16[1536,3584]{1,0:T(8,128)(2,1)} %param.6), kind=kOutput, calls=%fused_computation.15 | convolution fusion | flops 704643072 | bytes 11862016 | tf_op jit(solution)/shard_map/dot_general | solution.py:13
  132.1 5.9 %fusion = bf16[1536,3584]{0,1:T(8,128)(2,1)} fusion(bf16[64,3584]{1,0:T(8,128)(2,1)S(1)} %get-tuple-element.14, bf16[64,1536]{1,0:T(8,128)(2,1)S(1)} %all_gather.6), kind=kOutput, calls=%fused_computation.3 | convolution fusion | flops 710148096 | bytes 11665408 | tf_op jit(solution)/shard_map/dot_general | solution.py:19
  138.0 14.6 %copy.10 = bf16[1536,3584]{1,0:T(8,128)(2,1)} copy(bf16[1536,3584]{0,1:T(8,128)(2,1)} %fusion) | data formatting | bytes 22020096
  152.6 8.3 %convolution_add_fusion = f32[64,1536]{1,0:T(8,128)} fusion(f32[64,1536]{1,0:T(8,128)S(1)} %fusion.7, bf16[64,3584]{1,0:T(8,128)(2,1)S(1)} %get-tuple-element.13, bf16[1536,3584]{1,0:T(8,128)(2,1)} %param.7), kind=kOutput, calls=%fused_computation.5 | convolution fusion | flops 704741376 | bytes 12255232 | tf_op jit(solution)/shard_map/dot_general | solution.py:13
  160.9 0.0 reduce-scatter.5.cloned.1.call-update
  160.9 5.9 %fusion.1 = bf16[1536,3584]{0,1:T(8,128)(2,1)} fusion(bf16[64,3584]{1,0:T(8,128)(2,1)S(1)} %get-tuple-element.13, bf16[64,1536]{1,0:T(8,128)(2,1)S(1)} %all_gather.6), kind=kOutput, calls=%fused_computation.4 | convolution fusion | flops 710148096 | bytes 11665408 | tf_op jit(solution)/shard_map/dot_general | solution.py:19
  166.8 14.6 %copy.11 = bf16[1536,3584]{1,0:T(8,128)(2,1)} copy(bf16[1536,3584]{0,1:T(8,128)(2,1)} %fusion.1) | data formatting | bytes 22020096
  181.4 5.9 %convolution_convert_fusion = bf16[3584,1536]{1,0:T(8,128)(2,1)} fusion(bf16[64,3584]{1,0:T(8,128)(2,1)S(1)} %get-tuple-element.15, bf16[64,1536]{1,0:T(8,128)(2,1)S(1)} %all_gather.7), kind=kOutput, calls=%fused_computation | convolution fusion | flops 710148096 | bytes 11665408 | tf_op jit(solution)/shard_map/dot_general | solution.py:19
  187.3 1.5 convert_element_type.31
  188.8 1.5 convert_element_type.34
  (4 shorter events, 0.0 us)
Async XLA Ops:
  7.2 108.0 %all-reduce.3.cloned.1.call-start = ((), (), s32[]{:S(2)}) async-start(), calls=%async_computation.4 | async-start | bytes 5505024 | tf_op jit(solution)/shard_map/psum | solution.py:29
  7.2 23.0 %copy-start = (bf16[1536,3584]{1,0:T(8,128)(2,1)S(1)}, bf16[1536,3584]{1,0:T(8,128)(2,1)}, u32[]{:S(2)}) copy-start(bf16[1536,3584]{1,0:T(8,128)(2,1)} %param.6) | copy-start | bytes 33030148
  23.0 24.2 %slice-start = ((s8[11010048]{0:T(1024)(128)(4,1)}), s8[4194304]{0:T(1024)(128)(4,1)S(1)}, s32[]{:S(2)}) async-start(s8[11010048]{0:T(1024)(128)(4,1)} %bitcast.22), calls=%async_computation.5 | async-start | bytes 8388608
  23.0 24.2 %slice-start.1 = ((s8[11010048]{0:T(1024)(128)(4,1)}), s8[4194304]{0:T(1024)(128)(4,1)S(1)}, s32[]{:S(2)}) async-start(s8[11010048]{0:T(1024)(128)(4,1)} %bitcast.22), calls=%async_computation.6 | async-start | bytes 8388608
  30.2 3.0 %copy-start.1 = (bf16[16,1536]{1,0:T(8,128)(2,1)S(1)}, bf16[16,1536]{1,0:T(8,128)(2,1)}, u32[]{:S(2)}) copy-start(bf16[16,1536]{1,0:T(8,128)(2,1)} %param.9) | copy-start | bytes 147460
  30.2 17.0 %slice-start.2 = ((s8[11010048]{0:T(1024)(128)(4,1)}), s8[2621440]{0:T(1024)(128)(4,1)S(1)}, s32[]{:S(2)}) async-start(s8[11010048]{0:T(1024)(128)(4,1)} %bitcast.22), calls=%async_computation.7 | async-start | bytes 5242880
  51.6 135.7 %reduce-scatter.3.cloned.1.call-start = ((), (), s32[]{:S(2)}) async-start(), calls=%async_computation.2 | async-start | bytes 491520 | tf_op jit(solution)/shard_map/reduce_scatter | solution.py:33
  124.3 64.5 %reduce-scatter.5.cloned.1.call-start = ((), (), s32[]{:S(2)}) async-start(), calls=%async_computation.3 | async-start | bytes 491520 | tf_op jit(solution)/shard_map/reduce_scatter | solution.py:50
Sparse Core Ops, SparseCore 0:
  51.7 63.4 all-reduce.2
  124.4 20.6 reduce-scatter.2
  161.0 20.6 reduce-scatter.4
where the time goes:
time: 198 us; the launch traced here: 197 us
  waiting for transfers between devices  63.6 us (32%)
  matrix products  54.9 us (28%)
  blocking collectives  29.8 us (15%)
  local copies, waits for them, and re-layouts  29.3 us (15%)
  between operations  13.8 us (7%)
  other arithmetic  5.25 us (3%)
    psum x1, waiting for transfers between devices, local(): gate_pre, up_pre = lax.psum((gate_pre, up_pre), ('gy', 'gz'))  63.5 us
    unnamed x12, local copies, waits for them, and re-layouts  29.3 us
    dot_general x3, matrix products, inner_last(): lax.dot_general(left, right, (((1,), (1,)), ((), ())), preferred_element_...  20.1 us
    dot_general x3, matrix products, inner_first(): lax.dot_general(left, right, (((0,), (0,)), ((), ())), preferred_element_...  17.7 us
    all_gather x1, blocking collectives, local(): piece = lax.all_gather(tokens, 'gx', axis=0, tiled=True)  15.8 us
    all_gather x1, blocking collectives, local(): piece = lax.all_gather(grad_out, 'gx', axis=0, tiled=True)  14 us
    dot_general x1, matrix products, local(): up_pre = jnp.dot(piece, w_up, preferred_element_type=jnp.float32)  7.21 us
    dot_general x1, matrix products, local(): jnp.dot(rows_hidden, w_down, preferred_element_type=jnp.float32)  6.88 us
  transfers between devices with their start and end apart: 3, of which 1 were waited for; matrix products, arithmetic and copies ran while one was open for 33% of the time, Pallas kernels for 0%

commit v1 on v0

v1 whole, which is shorter than its diff:
```python
import functools

import jax
import jax.numpy as jnp
from jax import lax
from jax.experimental import pallas as pl
from jax.experimental.pallas import tpu as pltpu
from jax.sharding import PartitionSpec as P

MESH = pl.DeviceIdType.MESH
BF16 = jnp.bfloat16
F32 = jnp.float32
VMEM_BYTES = 58 * 2**20


def dot(left, right, dims=((1,), (0,))):
    return lax.dot_general(left, right, (dims, ((), ())), preferred_element_type=F32)


def chunk_of(width):
    return 512 if width % 512 == 0 else width


def remote(src, dst, send_sem, recv_sem, device):
    return pltpu.make_async_remote_copy(
        src_ref=src,
        dst_ref=dst,
        send_sem=send_sem,
        recv_sem=recv_sem,
        device_id=device,
        device_id_type=MESH,
    )


def main_kernel(
    n,
    m,
    tok_ref,
    cot_ref,
    wg_hbm,
    wu_hbm,
    wd_hbm,
    mixed_ref,
    gtok_ref,
    acts_ref,
    rows_ref,
    rows,
    wg,
    wu,
    wd,
    part,
    own,
    core_out,
    core_in,
    chip_out,
    chip_in,
    acts,
    mixed_acc,
    gtok_acc,
    scat_out,
    scat_in,
    w_sem,
    gather_send,
    gather_recv,
    core_send,
    core_recv,
    chip_send,
    chip_recv,
    acts_send,
    acts_recv,
    scat_send,
    scat_recv,
):
    me_x, me_y, me_z = (lax.axis_index(a) for a in ("gx", "gy", "gz"))
    other = 1 - me_z
    steps, depth, width = wg.shape
    block = tok_ref.shape[0]
    half = (n * block) // 2
    mine = pl.ds(pl.multiple_of(me_z * half, half), half)
    theirs = pl.ds(pl.multiple_of(other * half, half), half)

    def slab(index):
        return pl.ds(pl.multiple_of(index * block, block), block)

    def weight_copies(k):
        columns = pl.ds(pl.multiple_of(k * width, width), width)
        if steps == 1:
            columns = slice(None)
        return (
            pltpu.make_async_copy(wg_hbm.at[:, columns], wg.at[k], w_sem.at[k, 0]),
            pltpu.make_async_copy(wu_hbm.at[:, columns], wu.at[k], w_sem.at[k, 1]),
            pltpu.make_async_copy(wd_hbm.at[columns, :], wd.at[k], w_sem.at[k, 2]),
        )

    for k in range(steps):
        for copy in weight_copies(k):
            copy.start()

    barrier = pltpu.get_barrier_semaphore()
    for d in range(1, n):
        pl.semaphore_signal(
            barrier, inc=1, device_id={"gx": lax.rem(me_x + d, n)}, device_id_type=MESH
        )
    for d in range(1, m):
        pl.semaphore_signal(
            barrier, inc=1, device_id={"gy": lax.rem(me_y + d, m)}, device_id_type=MESH
        )
    pl.semaphore_signal(barrier, inc=1, device_id={"gz": other}, device_id_type=MESH)
    pl.semaphore_wait(barrier, n + m - 1)

    def gather_copy(a, d):
        src = tok_ref if a == 0 else cot_ref
        return remote(
            src,
            rows.at[a, slab(me_x)],
            gather_send.at[a, d],
            gather_recv.at[a, d],
            {"gx": lax.rem(me_x + d, n)},
        )

    for a in range(2):
        for d in range(1, n):
            gather_copy(a, d).start()
    rows[0, slab(me_x)] = tok_ref[...]
    rows[1, slab(me_x)] = cot_ref[...]
    mixed_acc[...] = jnp.zeros_like(mixed_acc)
    gtok_acc[...] = jnp.zeros_like(gtok_acc)
    for a in range(2):
        for d in range(1, n):
            gather_copy(a, d).wait()
    rows_ref[...] = rows[...]

    def core_copy(k):
        return remote(
            core_out.at[k], core_in.at[k], core_send.at[k], core_recv.at[k], {"gz": other}
        )

    def chip_copy(k, d):
        return remote(
            chip_out.at[k],
            chip_in.at[k, d - 1],
            chip_send.at[k, d],
            chip_recv.at[k, d],
            {"gy": lax.rem(me_y + d, m)},
        )

    def acts_copy(k):
        return remote(
            acts.at[k, :, mine],
            acts.at[k, :, mine],
            acts_send.at[k],
            acts_recv.at[k],
            {"gz": other},
        )

    def project(k):
        for copy in weight_copies(k):
            copy.wait()
        part[0] = dot(rows[0], wg[k])
        part[1] = dot(rows[0], wu[k])
        part[2] = dot(rows[1], wd[k], ((1,), (1,)))
        core_out[k] = part[:, theirs].astype(BF16)
        core_copy(k).start()
        own[k] = part[:, mine]

    def sum_cores(k):
        core_copy(k).wait()
        own[k] = own[k] + core_in[k].astype(F32)
        chip_out[k] = own[k].astype(BF16)
        for d in range(1, m):
            chip_copy(k, d).start()

    def activate(k):
        for d in range(1, m):
            chip_copy(k, d).wait()
        total = []
        for i in range(3):
            value = own[k, i]
            for d in range(1, m):
                value = value + chip_in[k, d - 1, i].astype(F32)
            total.append(value)
        gate, up, grad = total
        sig = jax.nn.sigmoid(gate)
        act = gate * sig
        acts[k, 0, mine] = (act * up).astype(BF16)
        acts[k, 1, mine] = (grad * up * (sig * (1.0 + gate * (1.0 - sig)))).astype(BF16)
        acts[k, 2, mine] = (grad * act).astype(BF16)
        acts_copy(k).start()

    tile = chunk_of(depth)

    def contract(k):
        acts_copy(k).wait()
        acts_ref[k] = acts[k]
        for t in range(0, depth, tile):
            span = slice(t, t + tile)
            mixed_acc[:, span] += dot(acts[k, 0], wd[k, :, span])
            gtok_acc[:, span] += dot(acts[k, 1], wg[k, span, :], ((1,), (1,)))
            gtok_acc[:, span] += dot(acts[k, 2], wu[k, span, :], ((1,), (1,)))

    def step(i, carry):
        for lag, stage in ((0, project), (1, sum_cores), (2, activate), (3, contract)):
            @pl.when(jnp.logical_and(i >= lag, i < steps + lag))
            def _():
                stage(i - lag)

        return carry

    lax.fori_loop(0, steps + 3, step, 0)

    def scatter_copy(d):
        return remote(
            scat_out.at[d],
            scat_in.at[d],
            scat_send.at[d],
            scat_recv.at[d],
            {"gx": lax.rem(me_x + d, n)},
        )

    for d in range(1, n):
        peer = slab(lax.rem(me_x + d, n))
        scat_out[d, 0] = mixed_acc[peer].astype(BF16)
        scat_out[d, 1] = gtok_acc[peer].astype(BF16)
        scatter_copy(d).start()
    mixed_sum = mixed_acc[slab(me_x)]
    gtok_sum = gtok_acc[slab(me_x)]
    for d in range(1, n):
        scatter_copy(d).wait()
        mixed_sum = mixed_sum + scat_in[d, 0].astype(F32)
        gtok_sum = gtok_sum + scat_in[d, 1].astype(F32)
    mixed_ref[...] = mixed_sum.astype(BF16)
    gtok_ref[...] = gtok_sum.astype(BF16)


def outer_kernel(acts_ref, rows_ref, gg_ref, gu_ref, gd_ref, tok_t):
    @pl.when(pl.program_id(0) == 0)
    def _():
        tok_t[...] = rows_ref[0].T

    depth, width = gg_ref.shape
    tile = 256 if depth % 256 == 0 else depth

    def body(t, carry):
        span = pl.ds(pl.multiple_of(t * tile, tile), tile)
        left = tok_t[span, :]
        gg_ref[span, :] = dot(left, acts_ref[0, 1]).astype(BF16)
        gu_ref[span, :] = dot(left, acts_ref[0, 2]).astype(BF16)
        gd_ref[:, span] = dot(acts_ref[0, 0], rows_ref[1, :, span], ((0,), (0,))).astype(BF16)
        return carry

    lax.fori_loop(0, depth // tile, body, 0)


def local(n, m, tokens, w_gate, w_up, w_down, grad_out):
    block, depth = tokens.shape
    ff = w_gate.shape[1]
    width = chunk_of(ff)
    steps = ff // width
    count = n * block
    half = count // 2
    vmem = pl.BlockSpec(memory_space=pltpu.VMEM)
    anywhere = pl.BlockSpec(memory_space=pl.ANY)
    dma = pltpu.SemaphoreType.DMA
    mixed, gtok, acts, rows = pl.pallas_call(
        functools.partial(main_kernel, n, m),
        out_shape=(
            jax.ShapeDtypeStruct((block, depth), BF16),
            jax.ShapeDtypeStruct((block, depth), BF16),
            jax.ShapeDtypeStruct((steps, 3, count, width), BF16),
            jax.ShapeDtypeStruct((2, count, depth), BF16),
        ),
        in_specs=[vmem, vmem, anywhere, anywhere, anywhere],
        out_specs=(vmem, vmem, vmem, vmem),
        scratch_shapes=[
            pltpu.VMEM((2, count, depth), BF16),
            pltpu.VMEM((steps, depth, width), BF16),
            pltpu.VMEM((steps, depth, width), BF16),
            pltpu.VMEM((steps, width, depth), BF16),
            pltpu.VMEM((3, count, width), F32),
            pltpu.VMEM((steps, 3, half, width), F32),
            pltpu.VMEM((steps, 3, half, width), BF16),
            pltpu.VMEM((steps, 3, half, width), BF16),
            pltpu.VMEM((steps, 3, half, width), BF16),
            pltpu.VMEM((steps, m - 1, 3, half, width), BF16),
            pltpu.VMEM((steps, 3, count, width), BF16),
            pltpu.VMEM((count, depth), F32),
            pltpu.VMEM((count, depth), F32),
            pltpu.VMEM((n, 2, block, depth), BF16),
            pltpu.VMEM((n, 2, block, depth), BF16),
            dma((steps, 3)),
            dma((2, n)),
            dma((2, n)),
            dma((steps,)),
            dma((steps,)),
            dma((steps, m)),
            dma((steps, m)),
            dma((steps,)),
            dma((steps,)),
            dma((n,)),
            dma((n,)),
        ],
        compiler_params=pltpu.CompilerParams(
            collective_id=0, has_side_effects=True, vmem_limit_bytes=VMEM_BYTES
        ),
    )(tokens, grad_out, w_gate, w_up, w_down)
    grad_gate, grad_up, grad_down = pl.pallas_call(
        outer_kernel,
        grid=(steps,),
        out_shape=(
            jax.ShapeDtypeStruct((depth, ff), BF16),
            jax.ShapeDtypeStruct((depth, ff), BF16),
            jax.ShapeDtypeStruct((ff, depth), BF16),
        ),
        in_specs=[
            pl.BlockSpec((1, 3, count, width), lambda k: (k, 0, 0, 0)),
            pl.BlockSpec((2, count, depth), lambda k: (0, 0, 0)),
        ],
        out_specs=(
            pl.BlockSpec((depth, width), lambda k: (0, k)),
            pl.BlockSpec((depth, width), lambda k: (0, k)),
            pl.BlockSpec((width, depth), lambda k: (k, 0)),
        ),
        scratch_shapes=[pltpu.VMEM((depth, count), BF16)],
        compiler_params=pltpu.CompilerParams(vmem_limit_bytes=VMEM_BYTES),
    )(acts, rows)
    return mixed, gtok, grad_gate, grad_up, grad_down


def solution(mesh):
    return jax.shard_map(
        functools.partial(local, mesh.shape["gx"], mesh.shape["gy"]),
        mesh=mesh,
        in_specs=(
            P(("grp", "gx"), ("gy", "gz")),
            P(("gy", "gz"), "gx"),
            P(("gy", "gz"), "gx"),
            P("gx", ("gy", "gz")),
            P(("grp", "gx"), ("gy", "gz")),
        ),
        out_specs=(
            P(("grp", "gx"), ("gy", "gz")),
            P(("grp", "gx"), ("gy", "gz")),
            P(("grp", "gy", "gz"), "gx"),
            P(("grp", "gy", "gz"), "gx"),
            P(("grp", "gx"), ("gy", "gz")),
        ),
        check_vma=False,
    )
```

time: 198 us -> 74.8 us (0.38)
  Pallas kernels: 0 us -> 71 us
  waiting for transfers between devices: 63.6 us -> 0 us
  matrix products: 54.9 us -> 0 us
  blocking collectives: 29.8 us -> 0 us
  local copies, waits for them, and re-layouts: 29.3 us -> 2.84 us
  between operations: 13.8 us -> 0.64 us
  other arithmetic: 5.25 us -> 0 us
    pallas_call x0 -> x2, Pallas kernels: none -> 71 us  [the longest x1 52.7 us: local(): pl.pallas_call(functools.partial(main_kernel, n, m), out_shape=(jax.Shape...]
    psum x1 -> x0, waiting for transfers between devices: 63.5 us -> none  [local(): gate_pre, up_pre = lax.psum((gate_pre, up_pre), ('gy', 'gz'))]
    dot_general x9 -> x0, matrix products: 54.9 us -> none  [the longest x3 20.1 us: inner_last(): lax.dot_general(left, right, (((1,), (1,)), ((), ())), preferred_element_...]
    all_gather x2 -> x0, blocking collectives: 29.8 us -> none  [the longest x1 15.8 us: local(): piece = lax.all_gather(tokens, 'gx', axis=0, tiled=True)]
    unnamed x12 -> x2, local copies, waits for them, and re-layouts: 29.3 us -> 2.84 us
    convert_element_type x3 -> x0, other arithmetic: 5.25 us -> none  [the longest x1 2.21 us: local(): pre_up = (grad_hidden * act_gate).astype(jnp.bfloat16)]
  transfers between devices with their start and end apart: 3 -> 0, of which waited for: 1 -> 0; matrix products, arithmetic and copies ran while one was open for 33% -> 0% of each run, Pallas kernels for 0% -> 0%
where the time goes in v1:
time: 74.8 us; the launch traced here: 74.5 us
  Pallas kernels  71 us (95%)
  local copies, waits for them, and re-layouts  2.84 us (4%)
    pallas_call x1, Pallas kernels, local(): pl.pallas_call(functools.partial(main_kernel, n, m), out_shape=(jax.Shape...  52.7 us
    pallas_call x1, Pallas kernels, local(): pl.pallas_call(outer_kernel, grid=(steps,), out_shape=(jax.ShapeDtypeStru...  18.3 us
    unnamed x2, local copies, waits for them, and re-layouts  2.84 us

profile of v1, /device:TPU:0, one launch (start us, length us, event | category | flops | bytes accessed | tf_op | source)
XLA Modules:
  0.0 74.5 jit_solution(18182063901621337456)
XLA Ops:
  0.6 52.7 %shard_map.92 = (bf16[16,1536]{1,0:T(8,128)(2,1)}, bf16[16,1536]{1,0:T(8,128)(2,1)}, bf16[7,3,64,512]{3,2,1,0:T(8,128)(2,1)}, bf16[2,64,1536]{2,1,0:T(8,128)(2,1)}) custom-call(bf16[16,1536]{1,0:T(8,128)(2,1)} %tok_ref.1, bf16[16,1536]{1,0:T(8,128)(2,1)} %cot_ref.1, bf16[1536,3584]{1,0:T(8,128)(2,1)} %wg_hbm.1, bf16[1536,3584]{1,0:T(8,128)(2,1)} %wu_hbm.1, ...), custom_call_target="tpu_custom_call" | custom-call | tf_op jit(solution)/shard_map/pallas_call | solution.py:264
  53.4 18.3 %shard_map.93 = (bf16[1536,3584]{1,0:T(8,128)(2,1)}, bf16[1536,3584]{1,0:T(8,128)(2,1)}, bf16[3584,1536]{1,0:T(8,128)(2,1)}) custom-call(bf16[7,3,64,512]{3,2,1,0:T(8,128)(2,1)} %get-tuple-element.14.acts_ref, bf16[2,64,1536]{2,1,0:T(8,128)(2,1)} %get-tuple-element.15.rows_ref), custom_call_target="tpu_custom_call" | custom-call | tf_op jit(solution)/shard_map/pallas_call | solution.py:306
  71.7 1.4 %copy.12 = bf16[16,1536]{1,0:T(8,128)(2,1)} copy(bf16[16,1536]{1,0:T(8,128)(2,1)} %get-tuple-element.24) | data formatting | bytes 98304
  73.1 1.4 %copy.13 = bf16[16,1536]{1,0:T(8,128)(2,1)} copy(bf16[16,1536]{1,0:T(8,128)(2,1)} %get-tuple-element.25) | data formatting | bytes 98304

commit v2 on v1

--- a/solution.py
+++ b/solution.py
@@ -118,137 +118,193 @@
             {"gx": lax.rem(me_x + d, n)},
         )
 
-    for a in range(2):
+    def gather_start(a):
         for d in range(1, n):
             gather_copy(a, d).start()
+
+    def gather_wait(a):
+        for d in range(1, n):
+            gather_copy(a, d).wait()
+
+    gather_start(0)
     rows[0, slab(me_x)] = tok_ref[...]
     rows[1, slab(me_x)] = cot_ref[...]
     mixed_acc[...] = jnp.zeros_like(mixed_acc)
     gtok_acc[...] = jnp.zeros_like(gtok_acc)
-    for a in range(2):
+    gather_wait(0)
+    gather_start(1)
+
+    parts = (slice(0, 2), slice(2, 3))
+    results = (slice(0, 1), slice(1, 3))
+
+    def core_copy(k, way):
+        return remote(
+            core_out.at[k, parts[way]],
+            core_in.at[k, parts[way]],
+            core_send.at[k, way],
+            core_recv.at[k, way],
+            {"gz": other},
+        )
+
+    def chip_copy(k, way, d):
+        return remote(
+            chip_out.at[k, parts[way]],
+            chip_in.at[k, d - 1, parts[way]],
+            chip_send.at[k, d, way],
+            chip_recv.at[k, d, way],
+            {"gy": lax.rem(me_y + d, m)},
+        )
+
+    def acts_copy(k, way):
+        half_acts = acts.at[k, results[way], mine]
+        return remote(
+            half_acts, half_acts, acts_send.at[k, way], acts_recv.at[k, way], {"gz": other}
+        )
+
+    def send_partial(k, way):
+        span = parts[way]
+        core_out[k, span] = part[span, theirs].astype(BF16)
+        core_copy(k, way).start()
+        own[k, span] = part[span, mine]
+
+    def project(k):
+        gate_copy, up_copy, _ = weight_copies(k)
+        gate_copy.wait()
+        part[0] = dot(rows[0], wg[k])
+        up_copy.wait()
+        part[1] = dot(rows[0], wu[k])
+        send_partial(k, 0)
+
+    def project_back(k):
+        @pl.when(k == 0)
+        def _():
+            gather_wait(1)
+
+        weight_copies(k)[2].wait()
+        part[2] = dot(rows[1], wd[k], ((1,), (1,)))
+        send_partial(k, 1)
+
+    def sum_cores(k, way):
+        span = parts[way]
+        core_copy(k, way).wait()
+        total = own[k, span] + core_in[k, span].astype(F32)
+        own[k, span] = total
+        chip_out[k, span] = total.astype(BF16)
+        for d in range(1, m):
+            chip_copy(k, way, d).start()
+
+    def sum_chips(k, way):
+        span = parts[way]
+        total = own[k, span]
+        for d in range(1, m):
+            chip_copy(k, way, d).wait()
+            total = total + chip_in[k, d - 1, span].astype(F32)
+        return total
+
+    def activate(k):
+        total = sum_chips(k, 0)
+        own[k, parts[0]] = total
+        gate, up = total[0], total[1]
+        acts[k, 0, mine] = (gate * jax.nn.sigmoid(gate) * up).astype(BF16)
+        acts_copy(k, 0).start()
+
+    def activate_back(k):
+        grad = sum_chips(k, 1)[0]
+        gate, up = own[k, 0], own[k, 1]
+        sig = jax.nn.sigmoid(gate)
+        acts[k, 1, mine] = (grad * up * (sig * (1.0 + gate * (1.0 - sig)))).astype(BF16)
+        acts[k, 2, mine] = (grad * (gate * sig)).astype(BF16)
+        acts_copy(k, 1).start()
+
+    def scatter_copy(d, a):
+        return remote(
+            scat_out.at[d, a],
+            scat_in.at[d, a],
+            scat_send.at[d, a],
+            scat_recv.at[d, a],
+            {"gx": lax.rem(me_x + d, n)},
+        )
+
+    def scatter(a, acc):
         for d in range(1, n):
-            gather_copy(a, d).wait()
-    rows_ref[...] = rows[...]
-
-    def core_copy(k):
-        return remote(
-            core_out.at[k], core_in.at[k], core_send.at[k], core_recv.at[k], {"gz": other}
-        )
-
-    def chip_copy(k, d):
-        return remote(
-            chip_out.at[k],
-            chip_in.at[k, d - 1],
-            chip_send.at[k, d],
-            chip_recv.at[k, d],
-            {"gy": lax.rem(me_y + d, m)},
-        )
-
-    def acts_copy(k):
-        return remote(
-            acts.at[k, :, mine],
-            acts.at[k, :, mine],
-            acts_send.at[k],
-            acts_recv.at[k],
-            {"gz": other},
-        )
-
-    def project(k):
-        for copy in weight_copies(k):
-            copy.wait()
-        part[0] = dot(rows[0], wg[k])
-        part[1] = dot(rows[0], wu[k])
-        part[2] = dot(rows[1], wd[k], ((1,), (1,)))
-        core_out[k] = part[:, theirs].astype(BF16)
-        core_copy(k).start()
-        own[k] = part[:, mine]
-
-    def sum_cores(k):
-        core_copy(k).wait()
-        own[k] = own[k] + core_in[k].astype(F32)
-        chip_out[k] = own[k].astype(BF16)
-        for d in range(1, m):
-            chip_copy(k, d).start()
-
-    def activate(k):
-        for d in range(1, m):
-            chip_copy(k, d).wait()
-        total = []
-        for i in range(3):
-            value = own[k, i]
-            for d in range(1, m):
-                value = value + chip_in[k, d - 1, i].astype(F32)
-            total.append(value)
-        gate, up, grad = total
-        sig = jax.nn.sigmoid(gate)
-        act = gate * sig
-        acts[k, 0, mine] = (act * up).astype(BF16)
-        acts[k, 1, mine] = (grad * up * (sig * (1.0 + gate * (1.0 - sig)))).astype(BF16)
-        acts[k, 2, mine] = (grad * act).astype(BF16)
-        acts_copy(k).start()
+            scat_out[d, a] = acc[slab(lax.rem(me_x + d, n))].astype(BF16)
+            scatter_copy(d, a).start()
+
+    def collect(a, acc, out_ref):
+        total = acc[slab(me_x)]
+        for d in range(1, n):
+            scatter_copy(d, a).wait()
+            total = total + scat_in[d, a].astype(F32)
+        out_ref[...] = total.astype(BF16)
 
     tile = chunk_of(depth)
 
     def contract(k):
-        acts_copy(k).wait()
+        acts_copy(k, 0).wait()
+        for t in range(0, depth, tile):
+            span = slice(t, t + tile)
+            mixed_acc[:, span] += dot(acts[k, 0], wd[k, :, span])
+
+        @pl.when(k == steps - 1)
+        def _():
+            scatter(0, mixed_acc)
+
+    def contract_back(k):
+        acts_copy(k, 1).wait()
         acts_ref[k] = acts[k]
         for t in range(0, depth, tile):
             span = slice(t, t + tile)
-            mixed_acc[:, span] += dot(acts[k, 0], wd[k, :, span])
-            gtok_acc[:, span] += dot(acts[k, 1], wg[k, span, :], ((1,), (1,)))
-            gtok_acc[:, span] += dot(acts[k, 2], wu[k, span, :], ((1,), (1,)))
+            gtok_acc[:, span] += dot(acts[k, 1], wg[k, span, :], ((1,), (1,))) + dot(
+                acts[k, 2], wu[k, span, :], ((1,), (1,))
+            )
+
+    stages = (
+        (0, project),
+        (1, lambda k: sum_cores(k, 0)),
+        (4, activate),
+        (6, contract),
+        (3, project_back),
+        (4, lambda k: sum_cores(k, 1)),
+        (7, activate_back),
+        (9, contract_back),
+    )
 
     def step(i, carry):
-        for lag, stage in ((0, project), (1, sum_cores), (2, activate), (3, contract)):
+        for lag, stage in stages:
             @pl.when(jnp.logical_and(i >= lag, i < steps + lag))
             def _():
                 stage(i - lag)
 
         return carry
 
-    lax.fori_loop(0, steps + 3, step, 0)
-
-    def scatter_copy(d):
-        return remote(
-            scat_out.at[d],
-            scat_in.at[d],
-            scat_send.at[d],
-            scat_recv.at[d],
-            {"gx": lax.rem(me_x + d, n)},
-        )
-
-    for d in range(1, n):
-        peer = slab(lax.rem(me_x + d, n))
-        scat_out[d, 0] = mixed_acc[peer].astype(BF16)
-        scat_out[d, 1] = gtok_acc[peer].astype(BF16)
-        scatter_copy(d).start()
-    mixed_sum = mixed_acc[slab(me_x)]
-    gtok_sum = gtok_acc[slab(me_x)]
-    for d in range(1, n):
-        scatter_copy(d).wait()
-        mixed_sum = mixed_sum + scat_in[d, 0].astype(F32)
-        gtok_sum = gtok_sum + scat_in[d, 1].astype(F32)
-    mixed_ref[...] = mixed_sum.astype(BF16)
-    gtok_ref[...] = gtok_sum.astype(BF16)
-
-
-def outer_kernel(acts_ref, rows_ref, gg_ref, gu_ref, gd_ref, tok_t):
+    lax.fori_loop(0, steps + 9, step, 0)
+
+    scatter(1, gtok_acc)
+    rows_ref[...] = rows[...]
+    collect(0, mixed_acc, mixed_ref)
+    collect(1, gtok_acc, gtok_ref)
+
+
+def outer_kernel(
+    acts_ref, rows_ref, mixed_in, gtok_in, mixed_ref, gtok_ref, gg_ref, gu_ref, gd_ref, tok_t, hid_t
+):
     @pl.when(pl.program_id(0) == 0)
     def _():
         tok_t[...] = rows_ref[0].T
+        mixed_ref[...] = mixed_in[...]
+        gtok_ref[...] = gtok_in[...]
 
     depth, width = gg_ref.shape
+    hid_t[...] = acts_ref[0, 0].T
     tile = 256 if depth % 256 == 0 else depth
-
-    def body(t, carry):
-        span = pl.ds(pl.multiple_of(t * tile, tile), tile)
-        left = tok_t[span, :]
-        gg_ref[span, :] = dot(left, acts_ref[0, 1]).astype(BF16)
-        gu_ref[span, :] = dot(left, acts_ref[0, 2]).astype(BF16)
-        gd_ref[:, span] = dot(acts_ref[0, 0], rows_ref[1, :, span], ((0,), (0,))).astype(BF16)
-        return carry
-
-    lax.fori_loop(0, depth // tile, body, 0)
+    for t in range(0, depth, tile):
+        span = slice(t, t + tile)
+        gg_ref[span, :] = dot(tok_t[span, :], acts_ref[0, 1]).astype(BF16)
+        gu_ref[span, :] = dot(tok_t[span, :], acts_ref[0, 2]).astype(BF16)
+    tile = 128 if width % 128 == 0 else width
+    for t in range(0, width, tile):
+        span = slice(t, t + tile)
+        gd_ref[span, :] = dot(hid_t[span, :], rows_ref[1]).astype(BF16)
 
 
 def local(n, m, tokens, w_gate, w_up, w_down, grad_out):
@@ -290,23 +346,25 @@
             dma((steps, 3)),
             dma((2, n)),
             dma((2, n)),
-            dma((steps,)),
-            dma((steps,)),
-            dma((steps, m)),
-            dma((steps, m)),
-            dma((steps,)),
-            dma((steps,)),
-            dma((n,)),
-            dma((n,)),
+            dma((steps, 2)),
+            dma((steps, 2)),
+            dma((steps, m, 2)),
+            dma((steps, m, 2)),
+            dma((steps, 2)),
+            dma((steps, 2)),
+            dma((n, 2)),
+            dma((n, 2)),
         ],
         compiler_params=pltpu.CompilerParams(
             collective_id=0, has_side_effects=True, vmem_limit_bytes=VMEM_BYTES
         ),
     )(tokens, grad_out, w_gate, w_up, w_down)
-    grad_gate, grad_up, grad_down = pl.pallas_call(
+    mixed, gtok, grad_gate, grad_up, grad_down = pl.pallas_call(
         outer_kernel,
         grid=(steps,),
         out_shape=(
+            jax.ShapeDtypeStruct((block, depth), BF16),
+            jax.ShapeDtypeStruct((block, depth), BF16),
             jax.ShapeDtypeStruct((depth, ff), BF16),
             jax.ShapeDtypeStruct((depth, ff), BF16),
             jax.ShapeDtypeStruct((ff, depth), BF16),
@@ -314,15 +372,19 @@
         in_specs=[
             pl.BlockSpec((1, 3, count, width), lambda k: (k, 0, 0, 0)),
             pl.BlockSpec((2, count, depth), lambda k: (0, 0, 0)),
+            pl.BlockSpec((block, depth), lambda k: (0, 0)),
+            pl.BlockSpec((block, depth), lambda k: (0, 0)),
         ],
         out_specs=(
+            pl.BlockSpec((block, depth), lambda k: (0, 0)),
+            pl.BlockSpec((block, depth), lambda k: (0, 0)),
             pl.BlockSpec((depth, width), lambda k: (0, k)),
             pl.BlockSpec((depth, width), lambda k: (0, k)),
             pl.BlockSpec((width, depth), lambda k: (k, 0)),
         ),
-        scratch_shapes=[pltpu.VMEM((depth, count), BF16)],
+        scratch_shapes=[pltpu.VMEM((depth, count), BF16), pltpu.VMEM((width, count), BF16)],
         compiler_params=pltpu.CompilerParams(vmem_limit_bytes=VMEM_BYTES),
-    )(acts, rows)
+    )(acts, rows, mixed, gtok)
     return mixed, gtok, grad_gate, grad_up, grad_down
 
 

time: 74.8 us -> 58.8 us (0.79)
  Pallas kernels: 71 us -> 58 us
  local copies, waits for them, and re-layouts: 2.84 us -> 0 us
    pallas_call x1, Pallas kernels: 52.7 us -> 44.2 us  [local(): pl.pallas_call(functools.partial(main_kernel, n, m), out_shape=(jax.Shape...]
    pallas_call x1, Pallas kernels: 18.3 us -> 13.9 us  [local(): pl.pallas_call(outer_kernel, grid=(steps,), out_shape=(jax.ShapeDtypeStru...]
    unnamed x2 -> x0, local copies, waits for them, and re-layouts: 2.84 us -> none
where the time goes in v2:
time: 58.8 us; the launch traced here: 58.7 us
  Pallas kernels  58 us (99%)
  between operations  0.64 us (1%)
    pallas_call x1, Pallas kernels, local(): pl.pallas_call(functools.partial(main_kernel, n, m), out_shape=(jax.Shape...  44.2 us
    pallas_call x1, Pallas kernels, local(): pl.pallas_call(outer_kernel, grid=(steps,), out_shape=(jax.ShapeDtypeStru...  13.9 us

profile of v2, /device:TPU:0, one launch (start us, length us, event | category | flops | bytes accessed | tf_op | source)
XLA Modules:
  0.0 58.7 jit_solution(13270100584288136869)
XLA Ops:
  0.6 44.2 %shard_map.92 = (bf16[16,1536]{1,0:T(8,128)(2,1)}, bf16[16,1536]{1,0:T(8,128)(2,1)}, bf16[7,3,64,512]{3,2,1,0:T(8,128)(2,1)}, bf16[2,64,1536]{2,1,0:T(8,128)(2,1)}) custom-call(bf16[16,1536]{1,0:T(8,128)(2,1)} %tok_ref.1, bf16[16,1536]{1,0:T(8,128)(2,1)} %cot_ref.1, bf16[1536,3584]{1,0:T(8,128)(2,1)} %wg_hbm.1, bf16[1536,3584]{1,0:T(8,128)(2,1)} %wu_hbm.1, ...), custom_call_target="tpu_custom_call" | custom-call | tf_op jit(solution)/shard_map/pallas_call | solution.py:320
  44.8 13.9 %shard_map.93 = (bf16[16,1536]{1,0:T(8,128)(2,1)}, bf16[16,1536]{1,0:T(8,128)(2,1)}, bf16[1536,3584]{1,0:T(8,128)(2,1)}, bf16[1536,3584]{1,0:T(8,128)(2,1)}, bf16[3584,1536]{1,0:T(8,128)(2,1)}) custom-call(bf16[7,3,64,512]{3,2,1,0:T(8,128)(2,1)} %get-tuple-element.9.acts_ref, bf16[2,64,1536]{2,1,0:T(8,128)(2,1)} %get-tuple-element.10.rows_ref, ...), custom_call_target="tpu_custom_call" | custom-call | tf_op jit(solution)/shard_map/pallas_call | solution.py:362
